TPU v7x, 32 devices: a whole 2x2x4 slice. The times are simulated.
32 devices in a mesh: pair: 2 (over x), row: 4 (over y, core), col: 4 (over z).
Axes of the slice: x: 2, y: 2, z: 4, core: 2. Of those that a mesh axis runs over, the one named last changes fastest.
Arguments:
- features: bfloat16 [2, 64, 64, 512], P('pair', None, 'row', 'col'), may hold values from -6 to 6
- offsets: int32 [2, 2, 64, 512], P('pair', None, 'row', 'col'), may hold values from -8 to 7
- fractions: int32 [2, 2, 64, 512], P('pair', None, 'row', 'col'), may hold values from 0 to 255
- tissue: int32 [2, 8, 64], P('pair', 'row', 'col'), may hold values 0 or 1
- w_first: bfloat16 [9, 64, 128], replicated, may hold values from -0.1875 to 0.1875
- w_second: bfloat16 [9, 64, 64], replicated, may hold values from -0.25 to 0.25
- head_weight: bfloat16 [2, 64], replicated, may hold values from -0.75 to 0.75
Outputs:
- warped_features: bfloat16 [2, 64, 64, 512], P('pair', None, 'row', 'col')
- motion_field: float32 [2, 2, 64, 512], P('pair', None, 'row', 'col')
All inputs are finite; a program needn't handle non-finite values. No bound on the sum of `tissue` on one device may be relied on, other than what follows from the above.
Results may differ from a plain program's by a relative error of at most 0.0056.
Values may be sent and summed in bfloat16 or wider, within the bound.
A program may use at most 64 MiB of HBM per device.

v0:
```python
import jax
import jax.numpy as jnp
from jax import lax
from jax.sharding import PartitionSpec as P

MAXS = 8
BLK = 8


frac_scale = 256.0


def swapped(value, axis, bit):
    mask = 2**bit
    pairs = [(source, source ^ mask) for source in range(lax.axis_size(axis))]
    return lax.ppermute(value, axis, pairs)


def padded_2(shard, sides, width):
    for axis, dim in sides:
        peers, length = (lax.axis_size(axis), shard.shape[dim])
        up = [(i, (i + 1) % peers) for i in range(peers - 1)]
        down = [(j, i) for i, j in up]
        last = lax.slice_in_dim(shard, length - width, length, axis=dim)
        leading = lax.slice_in_dim(shard, 0, width, axis=dim)
        before = lax.ppermute(last, axis, up)
        after = lax.ppermute(leading, axis, down)
        shard = jnp.concatenate([before, shard, after], axis=dim)
    return shard


def convolve(padded, weights, height, columns):
    summed = None
    for tap_index in range(9):
        row_shift = tap_index // 3
        col_shift = tap_index % 3
        window = padded[:, row_shift : row_shift + height, col_shift : col_shift + columns]
        window = window.reshape(padded.shape[0], height * columns)
        product = jnp.dot(weights[tap_index], window, preferred_element_type=jnp.float32)
        summed = product if summed is None else summed + product
    return summed.reshape(weights.shape[1], height, columns)


def sample(source, motion, margin, height, columns):
    stride = columns + 2 * margin
    grid_rows = lax.broadcasted_iota(jnp.int32, (height, columns), 0).astype(jnp.float32)
    grid_cols = lax.broadcasted_iota(jnp.int32, (height, columns), 1).astype(jnp.float32)
    place_row = grid_rows + motion[0] + margin
    place_col = grid_cols + motion[1] + margin
    floor_row = jnp.floor(place_row)
    floor_col = jnp.floor(place_col)
    frac_row = place_row - floor_row
    frac_col = place_col - floor_col
    base_index = floor_row.astype(jnp.int32) * stride + floor_col.astype(jnp.int32)
    flat_source = source.reshape(source.shape[0], -1)

    def fetch(step_size):
        picked = jnp.take(flat_source, (base_index + step_size).reshape(-1), axis=1, mode="clip")
        return picked.reshape(source.shape[0], height, columns).astype(jnp.float32)

    blended = (1.0 - frac_row) * (1.0 - frac_col) * fetch(0) + (1.0 - frac_row) * frac_col * fetch(
        1
    )
    blended = blended + frac_row * (1.0 - frac_col) * fetch(stride)
    blended = blended + frac_row * frac_col * fetch(stride + 1)
    return blended.astype(jnp.bfloat16)


def shards(features, offsets, fractions, tissue, w_first, w_second, head_weight):
    channels = features.shape[1]
    height = features.shape[2]
    columns = features.shape[3]
    margin = MAXS + 1
    own_features = features[0]
    partner = swapped(own_features, "pair", 0)
    joined = jnp.concatenate([own_features, partner], axis=0)
    source_band = padded_2(own_features, (("row", 1), ("col", 2)), margin)
    hidden_one = jax.nn.relu(
        convolve(padded_2(joined, (("row", 1), ("col", 2)), 1), w_first, height, columns)
    ).astype(jnp.bfloat16)
    padded_hidden = padded_2(hidden_one, (("row", 1), ("col", 2)), 1)
    hidden_two = jax.nn.relu(convolve(padded_hidden, w_second, height, columns)).astype(
        jnp.bfloat16
    )
    residual = jnp.tanh(
        jnp.dot(
            head_weight,
            hidden_two.reshape(channels, height * columns),
            preferred_element_type=jnp.float32,
        )
    )
    residual = residual.reshape(2, height, columns)
    coverage = jnp.repeat(jnp.repeat(tissue[0], BLK, axis=0), BLK, axis=1).astype(jnp.float32)
    motion = offsets[0].astype(jnp.float32) + fractions[0].astype(jnp.float32) / frac_scale
    motion = motion + coverage[None] * residual
    warped = sample(source_band, motion, margin, height, columns)
    return (warped[None], motion[None])


def solution(mesh):
    return jax.shard_map(
        shards,
        mesh=mesh,
        in_specs=(
            P("pair", None, "row", "col"),
            P("pair", None, "row", "col"),
            P("pair", None, "row", "col"),
            P("pair", "row", "col"),
            P(),
            P(),
            P(),
        ),
        out_specs=(P("pair", None, "row", "col"), P("pair", None, "row", "col")),
        check_vma=False,
    )
```

profile of v0, /device:TPU:0, one launch (start us, length us, event | category | flops | bytes accessed | tf_op | source)
XLA Modules:
  0.0 102.0 jit_solution(15690299716766851851)
XLA Ops:
  0.7 1.3 %copy.55 = bf16[1,64,16,128]{1,3,2,0:T(8,128)(2,1)S(1)} copy(bf16[1,64,16,128]{3,2,1,0:T(8,128)(2,1)} %param.7) | data formatting | bytes 524288 | tf_op args[0]
  1.9 3.0 %collective-permute-start = (bf16[64,16,128]{0,2,1:T(8,128)(2,1)S(1)}, bf16[64,16,128]{0,2,1:T(8,128)(2,1)S(1)}, u32[]{:S(2)}, u32[]{:S(2)}) collective-permute-start(bf16[64,16,128]{0,2,1:T(8,128)(2,1)S(1)} %bitcast.167), channel_id=1, source_target_pairs={{0,16},{16,0},{1,17},{17,1},{2,18},{18,2},{3,19},{19,3},{4,20},{20... | collective-permute-start | bytes 786440 | tf_op jit(solution)/shard_map/ppermute | solution.py:16
  5.0 1.3 %collective-permute-start.10 = (bf16[64,9,128]{0,2,1:T(8,128)(2,1)S(1)}, bf16[64,9,128]{0,2,1:T(8,128)(2,1)S(1)}, u32[]{:S(2)}, u32[]{:S(2)}) collective-permute-start(bf16[64,9,128]{0,2,1:T(8,128)(2,1)S(1)} %get-tuple-element.27), channel_id=1, source_target_pairs={{4,0},{8,4},{12,8},{5,1},{9,5},{13,9},{6,2},{10,6},{14,10},{7,3},{... | collective-permute-start | bytes 442376 | tf_op jit(solution)/shard_map/ppermute | solution.py:27
  6.3 3.0 %collective-permute-start.9 = (bf16[64,9,128]{0,2,1:T(8,128)(2,1)S(1)}, bf16[64,9,128]{0,2,1:T(8,128)(2,1)S(1)}, u32[]{:S(2)}, u32[]{:S(2)}) collective-permute-start(bf16[64,9,128]{0,2,1:T(8,128)(2,1)S(1)} %get-tuple-element.26), channel_id=1, source_target_pairs={{0,4},{4,8},{8,12},{1,5},{5,9},{9,13},{2,6},{6,10},{10,14},{3,7},{... | collective-permute-start | bytes 442376 | tf_op jit(solution)/shard_map/ppermute | solution.py:26
  9.5 1.0 %collective-permute-done.9 = bf16[64,9,128]{0,2,1:T(8,128)(2,1)S(1)} collective-permute-done((bf16[64,9,128]{0,2,1:T(8,128)(2,1)S(1)}, bf16[64,9,128]{0,2,1:T(8,128)(2,1)S(1)}, u32[]{:S(2)}, u32[]{:S(2)}) %collective-permute-start.9) | collective-permute-done | bytes 147488 | tf_op jit(solution)/shard_map/ppermute | solution.py:26
  10.7 3.5 %collective-permute-start.11 = (bf16[64,34,9]{0,1,2:T(8,128)(2,1)S(1)}, bf16[64,34,9]{0,1,2:T(8,128)(2,1)S(1)}, u32[]{:S(2)}, u32[]{:S(2)}) collective-permute-start(bf16[64,34,9]{0,1,2:T(8,128)(2,1)S(1)} %copy.61), channel_id=1, source_target_pairs={{0,1},{1,2},{2,3},{4,5},{5,6},{6,7},{8,9},{9,10},{10,11},{12,13},{... | collective-permute-start | bytes 117512 | tf_op jit(solution)/shard_map/ppermute | solution.py:26
  14.2 1.3 %collective-permute-start.12 = (bf16[64,34,9]{0,1,2:T(8,128)(2,1)S(1)}, bf16[64,34,9]{0,1,2:T(8,128)(2,1)S(1)}, u32[]{:S(2)}, u32[]{:S(2)}) collective-permute-start(bf16[64,34,9]{0,1,2:T(8,128)(2,1)S(1)} %copy.62), channel_id=1, source_target_pairs={{1,0},{2,1},{3,2},{5,4},{6,5},{7,6},{9,8},{10,9},{11,10},{13,12},{... | collective-permute-start | bytes 117512 | tf_op jit(solution)/shard_map/ppermute | solution.py:27
  15.5 1.4 %collective-permute-done = bf16[64,16,128]{0,2,1:T(8,128)(2,1)S(1)} collective-permute-done((bf16[64,16,128]{0,2,1:T(8,128)(2,1)S(1)}, bf16[64,16,128]{0,2,1:T(8,128)(2,1)S(1)}, u32[]{:S(2)}, u32[]{:S(2)}) %collective-permute-start) | collective-permute-done | bytes 262176 | tf_op jit(solution)/shard_map/ppermute | solution.py:16
  17.0 3.9 %collective-permute-start.1 = (bf16[128,1,128]{0,2,1:T(8,128)(2,1)S(1)}, bf16[128,1,128]{0,2,1:T(8,128)(2,1)S(1)}, u32[]{:S(2)}, u32[]{:S(2)}) collective-permute-start(bf16[128,1,128]{0,2,1:T(8,128)(2,1)S(1)} %get-tuple-element.12), channel_id=1, source_target_pairs={{0,4},{4,8},{8,12},{1,5},{5,9},{9,13},{2,6},{6,10},{10,14},{3,7},{... | collective-permute-start | bytes 98312 | tf_op jit(solution)/shard_map/ppermute | solution.py:26
  20.8 1.3 %collective-permute-start.2 = (bf16[128,1,128]{0,2,1:T(8,128)(2,1)S(1)}, bf16[128,1,128]{0,2,1:T(8,128)(2,1)S(1)}, u32[]{:S(2)}, u32[]{:S(2)}) collective-permute-start(bf16[128,1,128]{0,2,1:T(8,128)(2,1)S(1)} %get-tuple-element.13), channel_id=1, source_target_pairs={{4,0},{8,4},{12,8},{5,1},{9,5},{13,9},{6,2},{10,6},{14,10},{7,3},{... | collective-permute-start | bytes 98312 | tf_op jit(solution)/shard_map/ppermute | solution.py:27
  22.3 0.7 copy.63
  23.0 0.7 copy.64
  23.9 2.3 %collective-permute-done.2 = bf16[128,1,128]{0,2,1:T(8,128)(2,1)S(1)} collective-permute-done((bf16[128,1,128]{0,2,1:T(8,128)(2,1)S(1)}, bf16[128,1,128]{0,2,1:T(8,128)(2,1)S(1)}, u32[]{:S(2)}, u32[]{:S(2)}) %collective-permute-start.2) | collective-permute-done | bytes 32800 | tf_op jit(solution)/shard_map/ppermute | solution.py:27
  26.3 4.5 %collective-permute-start.3 = (bf16[128,18,1]{0,1,2:T(8,128)(2,1)S(1)}, bf16[128,18,1]{0,1,2:T(8,128)(2,1)S(1)}, u32[]{:S(2)}, u32[]{:S(2)}) collective-permute-start(bf16[128,18,1]{0,1,2:T(8,128)(2,1)S(1)} %copy.56), channel_id=1, source_target_pairs={{0,1},{1,2},{2,3},{4,5},{5,6},{6,7},{8,9},{9,10},{10,11},{12,13},{... | collective-permute-start | bytes 13832 | tf_op jit(solution)/shard_map/ppermute | solution.py:26
  30.9 1.3 %collective-permute-start.4 = (bf16[128,18,1]{0,1,2:T(8,128)(2,1)S(1)}, bf16[128,18,1]{0,1,2:T(8,128)(2,1)S(1)}, u32[]{:S(2)}, u32[]{:S(2)}) collective-permute-start(bf16[128,18,1]{0,1,2:T(8,128)(2,1)S(1)} %copy.58), channel_id=1, source_target_pairs={{1,0},{2,1},{3,2},{5,4},{6,5},{7,6},{9,8},{10,9},{11,10},{13,12},{... | collective-permute-start | bytes 13832 | tf_op jit(solution)/shard_map/ppermute | solution.py:27
  32.2 0.4 pad_maximum_fusion.3
  32.6 3.8 %collective-permute-done.4 = bf16[128,18,1]{0,1,2:T(8,128)(2,1)S(1)} collective-permute-done((bf16[128,18,1]{0,1,2:T(8,128)(2,1)S(1)}, bf16[128,18,1]{0,1,2:T(8,128)(2,1)S(1)}, u32[]{:S(2)}, u32[]{:S(2)}) %collective-permute-start.4) | collective-permute-done | bytes 4640 | tf_op jit(solution)/shard_map/ppermute | solution.py:27
  36.4 0.6 maximum_maximum_fusion.1
  37.1 0.6 fusion.79
  37.7 0.3 copy-done.7
  38.0 0.3 fusion.54
  38.3 0.3 fusion.46
  38.6 0.3 fusion.48
  38.9 0.3 fusion.43
  39.2 0.3 convolution_add_fusion.12
  39.5 0.3 convolution_add_fusion.11
  39.8 0.3 convolution_add_fusion.10
  40.1 0.2 fusion.3
  40.4 0.3 fusion.6
  40.7 0.7 fusion.83
  41.4 3.1 %collective-permute-start.5 = (bf16[64,1,128]{2,1,0:T(2,128)(2,1)}, bf16[64,1,128]{2,1,0:T(2,128)(2,1)S(1)}, u32[]{:S(2)}, u32[]{:S(2)}) collective-permute-start(bf16[64,1,128]{2,1,0:T(2,128)(2,1)} %get-tuple-element.34), channel_id=1, source_target_pairs={{0,4},{4,8},{8,12},{1,5},{5,9},{9,13},{2,6},{6,10},{10,14},{3,7},{... | collective-permute-start | bytes 49160 | tf_op jit(solution)/shard_map/ppermute | solution.py:26
  44.5 1.3 %collective-permute-start.6 = (bf16[64,1,128]{2,1,0:T(2,128)(2,1)S(1)}, bf16[64,1,128]{2,1,0:T(2,128)(2,1)S(1)}, u32[]{:S(2)}, u32[]{:S(2)}) collective-permute-start(bf16[64,1,128]{2,1,0:T(2,128)(2,1)S(1)} %get-tuple-element.35), channel_id=1, source_target_pairs={{4,0},{8,4},{12,8},{5,1},{9,5},{13,9},{6,2},{10,6},{14,10},{7,3},{... | collective-permute-start | bytes 49160 | tf_op jit(solution)/shard_map/ppermute | solution.py:27
  45.8 0.5 pad_maximum_fusion
  46.3 0.5 reshape.402
  46.8 2.0 %collective-permute-done.6 = bf16[64,1,128]{2,1,0:T(2,128)(2,1)S(1)} collective-permute-done((bf16[64,1,128]{2,1,0:T(2,128)(2,1)S(1)}, bf16[64,1,128]{2,1,0:T(2,128)(2,1)S(1)}, u32[]{:S(2)}, u32[]{:S(2)}) %collective-permute-start.6) | collective-permute-done | bytes 16416 | tf_op jit(solution)/shard_map/ppermute | solution.py:27
  48.7 0.2 pad_maximum_fusion.7
  49.1 3.5 %collective-permute-start.7 = (bf16[64,18,1]{2,1,0:T(8,128)(2,1)S(1)}, bf16[64,18,1]{2,1,0:T(8,128)(2,1)S(1)}, u32[]{:S(2)}, u32[]{:S(2)}) collective-permute-start(bf16[64,18,1]{2,1,0:T(8,128)(2,1)S(1)} %get-tuple-element.29), channel_id=1, source_target_pairs={{0,1},{1,2},{2,3},{4,5},{5,6},{6,7},{8,9},{9,10},{10,11},{12,13},{... | collective-permute-start | bytes 6920 | tf_op jit(solution)/shard_map/ppermute | solution.py:26
  52.6 1.5 %collective-permute-start.8 = (bf16[64,18,1]{2,1,0:T(8,128)(2,1)S(1)}, bf16[64,18,1]{2,1,0:T(8,128)(2,1)S(1)}, u32[]{:S(2)}, u32[]{:S(2)}) collective-permute-start(bf16[64,18,1]{2,1,0:T(8,128)(2,1)S(1)} %get-tuple-element.28), channel_id=1, source_target_pairs={{1,0},{2,1},{3,2},{5,4},{6,5},{7,6},{9,8},{10,9},{11,10},{13,12},{... | collective-permute-start | bytes 6920 | tf_op jit(solution)/shard_map/ppermute | solution.py:27
  54.1 0.3 pad_maximum_fusion.8
  54.4 6.0 %collective-permute-done.7 = bf16[64,18,1]{2,1,0:T(8,128)(2,1)S(1)} collective-permute-done((bf16[64,18,1]{2,1,0:T(8,128)(2,1)S(1)}, bf16[64,18,1]{2,1,0:T(8,128)(2,1)S(1)}, u32[]{:S(2)}, u32[]{:S(2)}) %collective-permute-start.7) | collective-permute-done | bytes 2336 | tf_op jit(solution)/shard_map/ppermute | solution.py:26
  60.4 4.7 %collective-permute-done.8 = bf16[64,18,1]{2,1,0:T(8,128)(2,1)S(1)} collective-permute-done((bf16[64,18,1]{2,1,0:T(8,128)(2,1)S(1)}, bf16[64,18,1]{2,1,0:T(8,128)(2,1)S(1)}, u32[]{:S(2)}, u32[]{:S(2)}) %collective-permute-start.8) | collective-permute-done | bytes 2336 | tf_op jit(solution)/shard_map/ppermute | solution.py:27
  65.1 1.1 %pad_maximum_fusion.1 = (bf16[64,18,129]{2,1,0:T(8,128)(2,1)S(1)}, bf16[64,18,129]{2,1,0:T(8,128)(2,1)S(1)}) fusion(bf16[64,18,1]{2,1,0:T(8,128)(2,1)S(1)} %collective-permute-done.8, bf16[64,1,128]{2,1,0:T(2,128)(2,1)S(1)} %collective-permute-done.6, bf16[64,16,128]{2,1,0:T(8,128)(2,1)S(1)} %bitcast.179, bf16[64,1,128]{2,1,0:T(2,128)(2,1)S(1)} %collective-permute-done.5, ...), kind=kLoop, calls=%fused_computation.28 | loop fusion | flops 2377728 | bytes 893952 | tf_op jit(solution)/shard_map/concatenate | solution.py:28
  66.4 0.4 fusion.77
  66.8 0.3 copy-done.8
  67.2 0.2 fusion.27
  67.4 0.2 convolution_add_fusion.7
  67.6 0.2 convolution_add_fusion.6
  67.8 0.2 convolution_add_fusion.5
  68.2 0.2 convolution_add_fusion.3
  68.5 0.2 convolution_add_fusion.2
  68.7 0.2 convolution_add_fusion.1
  68.9 0.3 fusion.7
  69.4 0.6 fusion.31
  70.3 6.2 %gather_fusion = bf16[2048,64]{1,0:T(8,128)(2,1)S(1)} fusion(bf16[64,4964]{0,1:T(8,128)(2,1)S(1)} %reshape.402, s32[2048]{0:T(1024)S(1)} %broadcast_clamp_fusion.3), kind=kCustom, calls=%fused_computation | custom fusion | bytes 532480 | tf_op jit(solution)/shard_map/jit(_take)/gather | solution.py:58
  76.5 0.4 copy.67
  76.9 6.2 %gather_fusion.1 = bf16[2048,64]{1,0:T(8,128)(2,1)S(1)} fusion(bf16[64,4964]{0,1:T(8,128)(2,1)S(1)} %reshape.402, s32[2048]{0:T(1024)S(1)} %broadcast_clamp_fusion.2), kind=kCustom, calls=%fused_computation.1 | custom fusion | bytes 532480 | tf_op jit(solution)/shard_map/jit(_take)/gather | solution.py:58
  83.2 0.4 copy.69
  83.6 8.0 %gather_fusion.2 = bf16[2048,64]{1,0:T(8,128)(2,1)} fusion(bf16[64,4964]{0,1:T(8,128)(2,1)S(1)} %reshape.402, s32[2048]{0:T(1024)S(1)} %broadcast_clamp_fusion.1), kind=kCustom, calls=%fused_computation.2 | custom fusion | bytes 532480 | tf_op jit(solution)/shard_map/jit(_take)/gather | solution.py:58
  91.7 1.1 %convert_element_type.187 = f32[2048,64]{1,0:T(8,128)S(1)} convert(bf16[2048,64]{1,0:T(8,128)(2,1)} %gather_fusion.2) | non-fusion elementwise | flops 131072 | bytes 786432 | tf_op jit(solution)/shard_map/convert_element_type | solution.py:59
  92.8 1.1 %copy.71 = f32[1,64,16,128]{3,2,1,0:T(8,128)} copy(f32[1,64,16,128]{1,3,2,0:T(8,128)S(1)} %bitcast.182) | data formatting | bytes 1048576 | tf_op jit(solution)/shard_map/convert_element_type | solution.py:59
  93.9 6.2 %gather_fusion.3 = bf16[2048,64]{1,0:T(8,128)(2,1)S(1)} fusion(bf16[64,4964]{0,1:T(8,128)(2,1)S(1)} %reshape.402, s32[2048]{0:T(1024)S(1)} %broadcast_clamp_fusion), kind=kCustom, calls=%fused_computation.3 | custom fusion | bytes 532480 | tf_op jit(solution)/shard_map/jit(_take)/gather | solution.py:58
  100.2 0.4 copy.73
  100.6 0.6 copy-done.1
  101.1 0.9 add_convert_fusion
  (63 shorter events, 2.1 us)
Async XLA Ops:
  0.6 68.3 %copy-start = (bf16[2,64]{1,0:T(2,128)(2,1)S(1)}, bf16[2,64]{1,0:T(2,128)(2,1)}, u32[]{:S(2)}) copy-start(bf16[2,64]{1,0:T(2,128)(2,1)} %param.13) | copy-start | bytes 772
  0.6 8.7 %copy-start.11 = (s32[1,2,16]{2,1,0:T(2,128)S(1)}, s32[1,2,16]{2,1,0:T(2,128)}, u32[]{:S(2)}) copy-start(s32[1,2,16]{2,1,0:T(2,128)} %param.10) | copy-start | bytes 388
  1.9 14.9 %collective-permute-start = (bf16[64,16,128]{0,2,1:T(8,128)(2,1)S(1)}, bf16[64,16,128]{0,2,1:T(8,128)(2,1)S(1)}, u32[]{:S(2)}, u32[]{:S(2)}) collective-permute-start(bf16[64,16,128]{0,2,1:T(8,128)(2,1)S(1)} %bitcast.167), channel_id=1, source_target_pairs={{0,16},{16,0},{1,17},{17,1},{2,18},{18,2},{3,19},{19,3},{4,20},{20... | collective-permute-start | bytes 786440 | tf_op jit(solution)/shard_map/ppermute | solution.py:16
  5.0 4.5 %collective-permute-start.10 = (bf16[64,9,128]{0,2,1:T(8,128)(2,1)S(1)}, bf16[64,9,128]{0,2,1:T(8,128)(2,1)S(1)}, u32[]{:S(2)}, u32[]{:S(2)}) collective-permute-start(bf16[64,9,128]{0,2,1:T(8,128)(2,1)S(1)} %get-tuple-element.27), channel_id=1, source_target_pairs={{4,0},{8,4},{12,8},{5,1},{9,5},{13,9},{6,2},{10,6},{14,10},{7,3},{... | collective-permute-start | bytes 442376 | tf_op jit(solution)/shard_map/ppermute | solution.py:27
  6.3 4.2 %collective-permute-start.9 = (bf16[64,9,128]{0,2,1:T(8,128)(2,1)S(1)}, bf16[64,9,128]{0,2,1:T(8,128)(2,1)S(1)}, u32[]{:S(2)}, u32[]{:S(2)}) collective-permute-start(bf16[64,9,128]{0,2,1:T(8,128)(2,1)S(1)} %get-tuple-element.26), channel_id=1, source_target_pairs={{0,4},{4,8},{8,12},{1,5},{5,9},{9,13},{2,6},{6,10},{10,14},{3,7},{... | collective-permute-start | bytes 442376 | tf_op jit(solution)/shard_map/ppermute | solution.py:26
  9.5 12.7 %copy-start.4 = (bf16[1,64,16,128]{3,2,1,0:T(8,128)(2,1)S(1)}, bf16[1,64,16,128]{3,2,1,0:T(8,128)(2,1)}, u32[]{:S(2)}) copy-start(bf16[1,64,16,128]{3,2,1,0:T(8,128)(2,1)} %param.7) | copy-start | bytes 786436
  10.6 6.4 %copy-start.2 = (bf16[64,9,128]{0,2,1:T(8,128)(2,1)}, bf16[64,9,128]{0,2,1:T(8,128)(2,1)S(1)}, u32[]{:S(2)}) copy-start(bf16[64,9,128]{0,2,1:T(8,128)(2,1)S(1)} %collective-permute-done.9) | copy-start | bytes 442372
  10.7 11.6 %collective-permute-start.11 = (bf16[64,34,9]{0,1,2:T(8,128)(2,1)S(1)}, bf16[64,34,9]{0,1,2:T(8,128)(2,1)S(1)}, u32[]{:S(2)}, u32[]{:S(2)}) collective-permute-start(bf16[64,34,9]{0,1,2:T(8,128)(2,1)S(1)} %copy.61), channel_id=1, source_target_pairs={{0,1},{1,2},{2,3},{4,5},{5,6},{6,7},{8,9},{9,10},{10,11},{12,13},{... | collective-permute-start | bytes 117512 | tf_op jit(solution)/shard_map/ppermute | solution.py:26
  14.2 8.8 %collective-permute-start.12 = (bf16[64,34,9]{0,1,2:T(8,128)(2,1)S(1)}, bf16[64,34,9]{0,1,2:T(8,128)(2,1)S(1)}, u32[]{:S(2)}, u32[]{:S(2)}) collective-permute-start(bf16[64,34,9]{0,1,2:T(8,128)(2,1)S(1)} %copy.62), channel_id=1, source_target_pairs={{1,0},{2,1},{3,2},{5,4},{6,5},{7,6},{9,8},{10,9},{11,10},{13,12},{... | collective-permute-start | bytes 117512 | tf_op jit(solution)/shard_map/ppermute | solution.py:27
  17.0 6.9 %collective-permute-start.1 = (bf16[128,1,128]{0,2,1:T(8,128)(2,1)S(1)}, bf16[128,1,128]{0,2,1:T(8,128)(2,1)S(1)}, u32[]{:S(2)}, u32[]{:S(2)}) collective-permute-start(bf16[128,1,128]{0,2,1:T(8,128)(2,1)S(1)} %get-tuple-element.12), channel_id=1, source_target_pairs={{0,4},{4,8},{8,12},{1,5},{5,9},{9,13},{2,6},{6,10},{10,14},{3,7},{... | collective-permute-start | bytes 98312 | tf_op jit(solution)/shard_map/ppermute | solution.py:26
  20.8 5.4 %collective-permute-start.2 = (bf16[128,1,128]{0,2,1:T(8,128)(2,1)S(1)}, bf16[128,1,128]{0,2,1:T(8,128)(2,1)S(1)}, u32[]{:S(2)}, u32[]{:S(2)}) collective-permute-start(bf16[128,1,128]{0,2,1:T(8,128)(2,1)S(1)} %get-tuple-element.13), channel_id=1, source_target_pairs={{4,0},{8,4},{12,8},{5,1},{9,5},{13,9},{6,2},{10,6},{14,10},{7,3},{... | collective-permute-start | bytes 98312 | tf_op jit(solution)/shard_map/ppermute | solution.py:27
  26.3 6.3 %collective-permute-start.3 = (bf16[128,18,1]{0,1,2:T(8,128)(2,1)S(1)}, bf16[128,18,1]{0,1,2:T(8,128)(2,1)S(1)}, u32[]{:S(2)}, u32[]{:S(2)}) collective-permute-start(bf16[128,18,1]{0,1,2:T(8,128)(2,1)S(1)} %copy.56), channel_id=1, source_target_pairs={{0,1},{1,2},{2,3},{4,5},{5,6},{6,7},{8,9},{9,10},{10,11},{12,13},{... | collective-permute-start | bytes 13832 | tf_op jit(solution)/shard_map/ppermute | solution.py:26
  30.9 5.5 %collective-permute-start.4 = (bf16[128,18,1]{0,1,2:T(8,128)(2,1)S(1)}, bf16[128,18,1]{0,1,2:T(8,128)(2,1)S(1)}, u32[]{:S(2)}, u32[]{:S(2)}) collective-permute-start(bf16[128,18,1]{0,1,2:T(8,128)(2,1)S(1)} %copy.58), channel_id=1, source_target_pairs={{1,0},{2,1},{3,2},{5,4},{6,5},{7,6},{9,8},{10,9},{11,10},{13,12},{... | collective-permute-start | bytes 13832 | tf_op jit(solution)/shard_map/ppermute | solution.py:27
  37.1 0.9 copy-start.7
  40.3 5.4 %copy-start.3 = (bf16[64,9,128]{0,2,1:T(8,128)(2,1)S(1)}, bf16[64,9,128]{0,2,1:T(8,128)(2,1)}, u32[]{:S(2)}) copy-start(bf16[64,9,128]{0,2,1:T(8,128)(2,1)} %copy-done.2) | copy-start | bytes 442372
  40.3 5.4 %copy-start.5 = (bf16[64,34,9]{0,2,1:T(8,128)(2,1)S(1)}, bf16[64,34,9]{0,2,1:T(8,128)(2,1)}, u32[]{:S(2)}) copy-start(bf16[64,34,9]{0,2,1:T(8,128)(2,1)} %copy.63) | copy-start | bytes 117508
  40.4 5.4 %copy-start.6 = (bf16[64,34,9]{0,2,1:T(8,128)(2,1)S(1)}, bf16[64,34,9]{0,2,1:T(8,128)(2,1)}, u32[]{:S(2)}) copy-start(bf16[64,34,9]{0,2,1:T(8,128)(2,1)} %copy.64) | copy-start | bytes 117508
  41.4 5.4 %collective-permute-start.5 = (bf16[64,1,128]{2,1,0:T(2,128)(2,1)}, bf16[64,1,128]{2,1,0:T(2,128)(2,1)S(1)}, u32[]{:S(2)}, u32[]{:S(2)}) collective-permute-start(bf16[64,1,128]{2,1,0:T(2,128)(2,1)} %get-tuple-element.34), channel_id=1, source_target_pairs={{0,4},{4,8},{8,12},{1,5},{5,9},{9,13},{2,6},{6,10},{10,14},{3,7},{... | collective-permute-start | bytes 49160 | tf_op jit(solution)/shard_map/ppermute | solution.py:26
  44.5 4.3 %collective-permute-start.6 = (bf16[64,1,128]{2,1,0:T(2,128)(2,1)S(1)}, bf16[64,1,128]{2,1,0:T(2,128)(2,1)S(1)}, u32[]{:S(2)}, u32[]{:S(2)}) collective-permute-start(bf16[64,1,128]{2,1,0:T(2,128)(2,1)S(1)} %get-tuple-element.35), channel_id=1, source_target_pairs={{4,0},{8,4},{12,8},{5,1},{9,5},{13,9},{6,2},{10,6},{14,10},{7,3},{... | collective-permute-start | bytes 49160 | tf_op jit(solution)/shard_map/ppermute | solution.py:27
  49.1 11.3 %collective-permute-start.7 = (bf16[64,18,1]{2,1,0:T(8,128)(2,1)S(1)}, bf16[64,18,1]{2,1,0:T(8,128)(2,1)S(1)}, u32[]{:S(2)}, u32[]{:S(2)}) collective-permute-start(bf16[64,18,1]{2,1,0:T(8,128)(2,1)S(1)} %get-tuple-element.29), channel_id=1, source_target_pairs={{0,1},{1,2},{2,3},{4,5},{5,6},{6,7},{8,9},{9,10},{10,11},{12,13},{... | collective-permute-start | bytes 6920 | tf_op jit(solution)/shard_map/ppermute | solution.py:26
  52.6 12.5 %collective-permute-start.8 = (bf16[64,18,1]{2,1,0:T(8,128)(2,1)S(1)}, bf16[64,18,1]{2,1,0:T(8,128)(2,1)S(1)}, u32[]{:S(2)}, u32[]{:S(2)}) collective-permute-start(bf16[64,18,1]{2,1,0:T(8,128)(2,1)S(1)} %get-tuple-element.28), channel_id=1, source_target_pairs={{1,0},{2,1},{3,2},{5,4},{6,5},{7,6},{9,8},{10,9},{11,10},{13,12},{... | collective-permute-start | bytes 6920 | tf_op jit(solution)/shard_map/ppermute | solution.py:27
  66.2 0.9 copy-start.8
  68.7 0.7 copy-start.9
  68.7 0.7 copy-start.10
  100.1 1.0 %copy-start.1 = (f32[1,64,16,128]{3,2,1,0:T(8,128)S(1)}, f32[1,64,16,128]{3,2,1,0:T(8,128)}, u32[]{:S(2)}) copy-start(f32[1,64,16,128]{3,2,1,0:T(8,128)} %copy.71) | copy-start | bytes 1572868
where the time goes:
time: 103 us; the launch traced here: 102 us
  local copies, waits for them, and re-layouts  36.1 us (35%)
  starting transfers between devices  32.5 us (32%)
  waiting for transfers between devices  21.2 us (21%)
  other arithmetic  6.34 us (6%)
  matrix products  4.63 us (4%)
  between operations  1.29 us (1%)
    gather x4, local copies, waits for them, and re-layouts, fetch(): jnp.take(flat_source, (base_index + step_size).reshape(-1), axis=1, mode=...  26.6 us
    ppermute x6, starting transfers between devices, padded_2(): before = lax.ppermute(last, axis, up)  21.5 us
    ppermute x6, waiting for transfers between devices, padded_2(): after = lax.ppermute(leading, axis, down)  12.8 us
    ppermute x6, starting transfers between devices, padded_2(): after = lax.ppermute(leading, axis, down)  7.93 us
    ppermute x6, waiting for transfers between devices, padded_2(): before = lax.ppermute(last, axis, up)  7.04 us
    dot_general x17, matrix products, convolve(): jnp.dot(weights[tap_index], window, preferred_element_type=jnp.float32)  4.3 us
    concatenate x6, other arithmetic, padded_2(): shard = jnp.concatenate([before, shard, after], axis=dim)  3.12 us
    ppermute x1, starting transfers between devices, swapped(): return lax.ppermute(value, axis, pairs)  3 us
  transfers between devices with their start and end apart: 13, of which 7 were waited for; matrix products, arithmetic and copies ran while one was open for 4% of the time, Pallas kernels for 0%

commit v1 on v0

v1 whole, which is shorter than its diff:
```python
import functools

import jax
import jax.numpy as jnp
from jax import lax
from jax.experimental import pallas as pl
from jax.experimental.pallas import tpu as pltpu
from jax.sharding import PartitionSpec as P

MAXS = 8
BLK = 8
MARGIN = MAXS + 1
FRAC_SCALE = 256.0
STRIP = 16
MESH = pl.DeviceIdType.MESH

STRIPS = [(dr, dc) for dr in (-1, 0, 1) for dc in (-1, 1)]
N_COPIES = 12


def lanes(shape):
    return lax.broadcasted_iota(jnp.int32, shape, len(shape) - 1)


def kernel(
    n_row,
    n_col,
    feat,
    offsets,
    fractions,
    tissue,
    w_first,
    w_second,
    head,
    out,
    motion_out,
    own,
    other,
    packed,
    strips,
    package,
    hidden,
    hidden_two,
    send_sem,
    recv_sem,
):
    height, channels, columns = feat.shape
    slots = columns // STRIP
    pair = lax.axis_index("pair")
    row = lax.axis_index("row")
    col = lax.axis_index("col")

    def exists(dr, dc):
        ok = None
        for test in (
            [row + dr >= 0, row + dr < n_row] if dr else []
        ) + ([col + dc >= 0, col + dc < n_col] if dc else []):
            ok = test if ok is None else jnp.logical_and(ok, test)
        return ok

    neighbours = [(dr, dc) for dr in (-1, 0, 1) for dc in (-1, 0, 1) if dr or dc]
    barrier = pltpu.get_barrier_semaphore()
    pl.semaphore_signal(
        barrier, inc=1, device_id=(1 - pair, row, col), device_id_type=MESH
    )
    expected = jnp.int32(1)
    for dr, dc in neighbours:
        here = exists(dr, dc)
        expected = expected + here.astype(jnp.int32)

        @pl.when(here)
        def _():
            pl.semaphore_signal(
                barrier, inc=1, device_id=(pair, row + dr, col + dc), device_id_type=MESH
            )

    lane = lanes((channels, columns))
    slot = lane // STRIP
    for plane in range(height // slots):
        first = jnp.zeros((channels, columns), jnp.float32)
        last = first
        for k in range(slots):
            value = feat[plane * slots + k].astype(jnp.float32)
            if k:
                value = pltpu.roll(value, STRIP * k, 1)
            first = jnp.where(slot == k, value, first)
            last = jnp.where(slot == (k - 1) % slots, value, last)
        packed[0, plane] = first.astype(jnp.bfloat16)
        packed[1, plane] = last.astype(jnp.bfloat16)

    pl.semaphore_wait(barrier, expected)

    def copy(index, source, target, device):
        return pltpu.make_async_remote_copy(
            src_ref=source,
            dst_ref=target,
            send_sem=send_sem.at[index],
            recv_sem=recv_sem.at[index],
            device_id=device,
            device_id_type=MESH,
        )

    partner = (1 - pair, row, col)
    low = pl.ds(0, columns)
    to_partner = copy(0, feat, other.at[pl.ds(2, height), :, low], partner)
    near = []
    for n, (dr, dc) in enumerate(STRIPS):
        near.append(
            (
                copy(
                    3 + n,
                    packed.at[0 if dc < 0 else 1],
                    strips.at[n],
                    (pair, row + dr, col + dc),
                ),
                (dr, dc),
                strips.at[n],
            )
        )
    for index, dr, source, target in (
        (1, 1, pl.ds(height - MARGIN, MARGIN), pl.ds(0, MARGIN)),
        (2, -1, pl.ds(0, MARGIN), pl.ds(height + MARGIN, MARGIN)),
    ):
        place = own.at[target, :, low]
        near.append((copy(index, feat.at[source], place, (pair, row + dr, col)), (dr, 0), place))

    for moved, (dr, dc), _ in near:
        pl.when(exists(dr, dc))(moved.start)
    to_partner.start()
    for _, (dr, dc), place in near:

        @pl.when(jnp.logical_not(exists(-dr, -dc)))
        def _():
            place[...] = jnp.zeros(place.shape, place.dtype)

    own[pl.ds(MARGIN, height), :, low] = feat[...]

    w_one = jnp.concatenate([w_first[pl.ds(192 * a, 192), :] for a in range(3)], axis=1)
    w_two = jnp.concatenate([w_second[pl.ds(192 * a, 192), :] for a in range(3)], axis=1)

    for moved, (dr, dc), _ in near:
        pl.when(exists(-dr, -dc))(moved.wait_recv)

    bundle = jnp.zeros((channels, columns), jnp.float32)
    for i in range(height + 2 * MARGIN):
        side = -1 if i < MARGIN else (0 if i < MARGIN + height else 1)
        k = i - MARGIN - side * height
        left = strips[STRIPS.index((-side, 1)), k // slots].astype(jnp.float32)
        right = strips[STRIPS.index((-side, -1)), k // slots].astype(jnp.float32)
        k = k % slots
        value = jnp.where(
            slot == k, right, jnp.where(slot == (k - 1) % slots, left, 0.0)
        )
        if k:
            value = pltpu.roll(value, columns - STRIP * k, 1)
        own[i, :, pl.ds(columns, columns)] = value.astype(jnp.bfloat16)
        j = i - MARGIN + 2
        if 0 <= j < height + 4:
            bundle = jnp.where(lane // 4 == j, pltpu.roll(value, 2 + 4 * j, 1), bundle)
    package[0] = bundle.astype(jnp.bfloat16)

    passed = [
        copy(9, package.at[0], package.at[1], partner),
        copy(
            10,
            own.at[pl.ds(MARGIN - 2, 2), :, low],
            other.at[pl.ds(0, 2), :, low],
            partner,
        ),
        copy(
            11,
            own.at[pl.ds(MARGIN + height, 2), :, low],
            other.at[pl.ds(height + 2, 2), :, low],
            partner,
        ),
    ]
    for moved in passed:
        moved.start()
    to_partner.wait_recv()
    for moved in passed:
        moved.wait_recv()
    bundle = package[1].astype(jnp.float32)
    for j in range(height + 4):
        other[j, :, pl.ds(columns, columns)] = pltpu.roll(
            bundle, (2 * columns - 2 - 4 * j) % columns, 1
        ).astype(jnp.bfloat16)

    wide = 2 * columns

    def joined_taps(z):
        return (
            pltpu.roll(z[:channels], 1, 1)
            + z[channels : 2 * channels]
            + pltpu.roll(z[2 * channels :], wide - 1, 1)
        )

    wide_lane = lanes((channels, wide))
    place_col = jnp.where(wide_lane < wide * 3 // 4, wide_lane, wide_lane - wide) + col * columns
    col_ok = jnp.logical_and(place_col >= 0, place_col < n_col * columns)

    def first_layer(step, carry):
        for part in range(3):
            y = step * 3 + part
            window = jnp.concatenate(
                [
                    piece
                    for a in range(3)
                    for piece in (own[y + MARGIN - 2 + a], other[y + a])
                ],
                axis=0,
            )
            value = joined_taps(jnp.dot(w_one, window, preferred_element_type=jnp.float32))
            place_row = row * height + y - 1
            row_ok = jnp.logical_and(place_row >= 0, place_row < n_row * height)
            ok = jnp.logical_and(col_ok, row_ok)
            hidden[y] = jnp.where(ok, jnp.maximum(value, 0.0), 0.0).astype(jnp.bfloat16)
        return carry

    lax.fori_loop(0, (height + 2) // 3, first_layer, 0)

    for y in range(height):
        window = jnp.concatenate([hidden[y + a] for a in range(3)], axis=0)
        value = joined_taps(jnp.dot(w_two, window, preferred_element_type=jnp.float32))
        hidden_two[:, pl.ds(y * columns, columns)] = jnp.maximum(value[:, :columns], 0.0).astype(
            jnp.bfloat16
        )

    residual = jnp.tanh(
        jnp.dot(head[...], hidden_two[...], preferred_element_type=jnp.float32)
    )
    cells = columns // BLK
    spread = (
        lax.broadcasted_iota(jnp.int32, (cells, columns), 1) // BLK
        == lax.broadcasted_iota(jnp.int32, (cells, columns), 0)
    ).astype(jnp.bfloat16)
    coverage = jnp.dot(
        tissue[...].astype(jnp.float32).astype(jnp.bfloat16),
        spread,
        preferred_element_type=jnp.float32,
    )
    for y in range(height):
        cover = coverage[y // BLK : y // BLK + 1]
        for k in range(2):
            motion_out[k, pl.ds(y, 1), :] = (
                offsets[k, pl.ds(y, 1), :].astype(jnp.float32)
                + fractions[k, pl.ds(y, 1), :].astype(jnp.float32) / FRAC_SCALE
                + cover * residual[k : k + 1, y * columns : (y + 1) * columns]
            )

    depth = 2 * MARGIN + 2
    source = lax.broadcasted_iota(jnp.int32, (wide, wide), 0)
    source = jnp.where(source < wide * 3 // 4, source, source - wide).astype(jnp.float32)
    target = lanes((1, wide))
    target_col = (target % columns).astype(jnp.float32)
    target_row = (target // columns).astype(jnp.float32)
    reach = lax.broadcasted_iota(jnp.int32, (depth, wide), 0).astype(jnp.float32) - MARGIN

    def warp(t, carry):
        y = 2 * t
        both = [
            jnp.concatenate(
                [motion_out[k, pl.ds(y, 1), :], motion_out[k, pl.ds(y + 1, 1), :]], axis=1
            )
            for k in range(2)
        ]
        col_weight = jnp.maximum(1.0 - jnp.abs(both[1] + target_col - source), 0.0)
        row_weight = jnp.maximum(1.0 - jnp.abs(both[0] + target_row - reach), 0.0)
        rows = own[pl.ds(y, depth)].reshape(depth * channels, wide)
        picked = jnp.dot(
            rows, col_weight.astype(jnp.bfloat16), preferred_element_type=jnp.float32
        )
        total = None
        for d in range(depth):
            term = picked[d * channels : (d + 1) * channels] * row_weight[d : d + 1]
            total = term if total is None else total + term
        total = total.astype(jnp.bfloat16)
        out[y] = total[:, :columns]
        out[y + 1] = total[:, columns:]
        return carry

    lax.fori_loop(0, height // 2, warp, 0)

    for moved, (dr, dc), _ in near:
        pl.when(exists(dr, dc))(moved.wait_send)
    to_partner.wait_send()
    for moved in passed:
        moved.wait_send()


def shards(n_row, n_col, features, offsets, fractions, tissue, w_first, w_second, head_weight):
    _, channels, height, columns = features.shape
    feat = jnp.transpose(features[0], (1, 0, 2))
    wide = 2 * columns
    vmem = pl.BlockSpec(memory_space=pltpu.VMEM)
    warped, motion = pl.pallas_call(
        functools.partial(kernel, n_row, n_col),
        out_shape=(
            jax.ShapeDtypeStruct((height, channels, columns), jnp.bfloat16),
            jax.ShapeDtypeStruct((2, height, columns), jnp.float32),
        ),
        in_specs=[vmem] * 7,
        out_specs=(vmem, vmem),
        scratch_shapes=[
            pltpu.VMEM((height + 2 * MARGIN, channels, wide), jnp.bfloat16),
            pltpu.VMEM((height + 4, channels, wide), jnp.bfloat16),
            pltpu.VMEM((2, 2, channels, columns), jnp.bfloat16),
            pltpu.VMEM((6, 2, channels, columns), jnp.bfloat16),
            pltpu.VMEM((2, channels, columns), jnp.bfloat16),
            pltpu.VMEM((height + 2, channels, wide), jnp.bfloat16),
            pltpu.VMEM((channels, height * columns), jnp.bfloat16),
            pltpu.SemaphoreType.DMA((N_COPIES,)),
            pltpu.SemaphoreType.DMA((N_COPIES,)),
        ],
        compiler_params=pltpu.CompilerParams(
            collective_id=0, has_side_effects=True, vmem_limit_bytes=48 * 1024 * 1024
        ),
        cost_estimate=pl.CostEstimate(
            flops=4 * 10**9, bytes_accessed=2 * 10**6, transcendentals=4096
        ),
    )(
        feat,
        offsets[0],
        fractions[0],
        tissue[0],
        w_first.reshape(-1, w_first.shape[-1]),
        w_second.reshape(-1, w_second.shape[-1]),
        head_weight,
    )
    return (jnp.transpose(warped, (1, 0, 2))[None], motion[None])


def solution(mesh):
    tile = P("pair", None, "row", "col")
    return jax.shard_map(
        functools.partial(shards, mesh.shape["row"], mesh.shape["col"]),
        mesh=mesh,
        in_specs=(tile, tile, tile, P("pair", "row", "col"), P(), P(), P()),
        out_specs=(tile, tile),
        check_vma=False,
    )
```

time: 103 us -> 23.9 us (0.23)
  local copies, waits for them, and re-layouts: 36.1 us -> 3.2 us
  starting transfers between devices: 32.5 us -> 0 us
  waiting for transfers between devices: 21.2 us -> 0 us
  Pallas kernels: 0 us -> 19.8 us
  other arithmetic: 6.34 us -> 0 us
  matrix products: 4.63 us -> 0 us
    ppermute x13 -> x0, starting transfers between devices: 32.5 us -> none  [the longest x6 21.5 us: padded_2(): before = lax.ppermute(last, axis, up)]
    gather x4 -> x0, local copies, waits for them, and re-layouts: 26.6 us -> none  [fetch(): jnp.take(flat_source, (base_index + step_size).reshape(-1), axis=1, mode=...]
    ppermute x13 -> x0, waiting for transfers between devices: 21.2 us -> none  [the longest x6 12.8 us: padded_2(): after = lax.ppermute(leading, axis, down)]
    pallas_call x0 -> x1, Pallas kernels: none -> 19.8 us  [shards(): pl.pallas_call(functools.partial(kernel, n_row, n_col), out_shape=(jax.Sh...]
    dot_general x18 -> x0, matrix products: 4.63 us -> none  [the longest x17 4.3 us: convolve(): jnp.dot(weights[tap_index], window, preferred_element_type=jnp.float32)]
    concatenate x6 -> x0, other arithmetic: 3.12 us -> none  [padded_2(): shard = jnp.concatenate([before, shard, after], axis=dim)]
    convert_element_type x8 -> x0, local copies, waits for them, and re-layouts: 2.43 us -> none  [the longest x4 2.3 us: fetch(): return picked.reshape(source.shape[0], height, columns).astype(jnp.float32)]
    convert_element_type x8 -> x0, other arithmetic: 2.18 us -> none  [the longest x4 1.32 us: fetch(): return picked.reshape(source.shape[0], height, columns).astype(jnp.float32)]
  transfers between devices with their start and end apart: 13 -> 0, of which waited for: 7 -> 0; matrix products, arithmetic and copies ran while one was open for 4% -> 0% of each run, Pallas kernels for 0% -> 0%
where the time goes in v1:
time: 23.9 us; the launch traced here: 23.8 us
  Pallas kernels  19.8 us (83%)
  local copies, waits for them, and re-layouts  3.2 us (13%)
  between operations  0.72 us (3%)
    pallas_call x1, Pallas kernels, shards(): pl.pallas_call(functools.partial(kernel, n_row, n_col), out_shape=(jax.Sh...  19.8 us
    unnamed x15, local copies, waits for them, and re-layouts  3.2 us

profile of v1, /device:TPU:0, one launch (start us, length us, event | category | flops | bytes accessed | tf_op | source)
XLA Modules:
  0.0 23.8 jit_solution(3513209328574358567)
XLA Ops:
  0.6 0.0 copy-start
  0.6 0.0 copy-start.1
  0.7 0.0 copy-start.2
  0.7 0.0 copy-start.3
  0.7 1.1 %copy.12 = bf16[1,64,16,128]{3,1,2,0:T(8,128)(2,1)S(1)} copy(bf16[1,64,16,128]{3,2,1,0:T(8,128)(2,1)} %param.7) | data formatting | bytes 524288 | tf_op args[0]
  1.7 0.0 copy-start.4
  1.8 0.0 copy-start.5
  1.8 0.0 copy-done
  1.8 0.0 copy-done.1
  1.8 0.0 copy-done.2
  1.8 0.0 copy-done.3
  1.8 0.6 %copy-done.4 = s32[1,2,16]{2,1,0:T(2,128)S(1)} copy-done((s32[1,2,16]{2,1,0:T(2,128)S(1)}, s32[1,2,16]{2,1,0:T(2,128)}, u32[]{:S(2)}) %copy-start.4) | copy-done | bytes 152
  2.4 0.0 copy-done.5
  2.4 19.8 %shard_map.86 = (bf16[16,64,128]{2,1,0:T(8,128)(2,1)S(1)}, f32[2,16,128]{2,1,0:T(8,128)S(1)}) custom-call(bf16[16,64,128]{2,1,0:T(8,128)(2,1)S(1)} %bitcast.15, s32[2,16,128]{2,1,0:T(8,128)S(1)} %bitcast.19, s32[2,16,128]{2,1,0:T(8,128)S(1)} %bitcast.20, s32[2,16]{1,0:T(2,128)S(1)} %bitcast.21, bf16[576,128]{1,0:T(8,128)(2,1)S(1)} %bitcast.17, ...), custom_call_target="tpu_custom_call" | custom-call | flops 4000000000 | bytes 2000000 | tf_op jit(solution)/shard_map/pallas_call | solution.py:295
  22.3 0.9 %copy.10 = bf16[1,64,16,128]{3,2,1,0:T(8,128)(2,1)} copy(bf16[1,64,16,128]{3,1,2,0:T(8,128)(2,1)S(1)} %bitcast.14) | data formatting | bytes 524288
  23.2 0.6 %copy.14 = f32[1,2,16,128]{3,2,1,0:T(8,128)} copy(f32[1,2,16,128]{3,2,1,0:T(8,128)S(1)} %bitcast.16) | data formatting | bytes 32768
Async XLA Ops:
  0.6 1.1 %copy-start = (bf16[9,64,128]{2,1,0:T(8,128)(2,1)S(1)}, bf16[9,64,128]{2,1,0:T(8,128)(2,1)}, u32[]{:S(2)}) copy-start(bf16[9,64,128]{2,1,0:T(8,128)(2,1)} %param.11) | copy-start | bytes 442372
  0.6 1.1 %copy-start.1 = (bf16[9,64,64]{2,1,0:T(8,128)(2,1)S(1)}, bf16[9,64,64]{2,1,0:T(8,128)(2,1)}, u32[]{:S(2)}) copy-start(bf16[9,64,64]{2,1,0:T(8,128)(2,1)} %param.12) | copy-start | bytes 221188
  0.7 1.1 %copy-start.2 = (s32[1,2,16,128]{3,2,1,0:T(8,128)S(1)}, s32[1,2,16,128]{3,2,1,0:T(8,128)}, u32[]{:S(2)}) copy-start(s32[1,2,16,128]{3,2,1,0:T(8,128)} %param.8) | copy-start | bytes 49156
  0.7 1.1 %copy-start.3 = (s32[1,2,16,128]{3,2,1,0:T(8,128)S(1)}, s32[1,2,16,128]{3,2,1,0:T(8,128)}, u32[]{:S(2)}) copy-start(s32[1,2,16,128]{3,2,1,0:T(8,128)} %param.9) | copy-start | bytes 49156
  1.7 0.7 %copy-start.4 = (s32[1,2,16]{2,1,0:T(2,128)S(1)}, s32[1,2,16]{2,1,0:T(2,128)}, u32[]{:S(2)}) copy-start(s32[1,2,16]{2,1,0:T(2,128)} %param.10) | copy-start | bytes 388
  1.8 0.7 %copy-start.5 = (bf16[2,64]{1,0:T(2,128)(2,1)S(1)}, bf16[2,64]{1,0:T(2,128)(2,1)}, u32[]{:S(2)}) copy-start(bf16[2,64]{1,0:T(2,128)(2,1)} %head.1) | copy-start | bytes 772

commit v2 on v1

--- a/solution.py
+++ b/solution.py
@@ -15,7 +15,8 @@
 MESH = pl.DeviceIdType.MESH
 
 STRIPS = [(dr, dc) for dr in (-1, 0, 1) for dc in (-1, 1)]
-N_COPIES = 12
+N_COPIES = 16
+CHUNKS = 4
 
 
 def lanes(shape):
@@ -25,12 +26,12 @@
 def kernel(
     n_row,
     n_col,
-    feat,
-    offsets,
-    fractions,
+    feat_in,
+    offsets_in,
+    fractions_in,
+    w_first_in,
+    w_second_in,
     tissue,
-    w_first,
-    w_second,
     head,
     out,
     motion_out,
@@ -41,10 +42,33 @@
     package,
     hidden,
     hidden_two,
+    partial,
+    flat,
+    feat,
+    feat_here,
+    offsets,
+    fractions,
+    w_first,
+    w_second,
     send_sem,
     recv_sem,
+    load_sem,
 ):
     height, channels, columns = feat.shape
+    loads = [
+        pltpu.make_async_copy(source, target, load_sem.at[n])
+        for n, (source, target) in enumerate(
+            (
+                (feat_in, feat_here),
+                (w_first_in, w_first),
+                (w_second_in, w_second),
+                (offsets_in, offsets),
+                (fractions_in, fractions),
+            )
+        )
+    ]
+    for load in loads:
+        load.start()
     slots = columns // STRIP
     pair = lax.axis_index("pair")
     row = lax.axis_index("row")
@@ -74,13 +98,18 @@
                 barrier, inc=1, device_id=(pair, row + dr, col + dc), device_id_type=MESH
             )
 
+    loads[0].wait()
+    flat[...] = feat_here[...].astype(jnp.float32).reshape(channels * height, columns)
+
     lane = lanes((channels, columns))
     slot = lane // STRIP
     for plane in range(height // slots):
         first = jnp.zeros((channels, columns), jnp.float32)
         last = first
         for k in range(slots):
-            value = feat[plane * slots + k].astype(jnp.float32)
+            y = plane * slots + k
+            value = flat[pl.ds(y, channels, stride=height), :]
+            feat[y] = value.astype(jnp.bfloat16)
             if k:
                 value = pltpu.roll(value, STRIP * k, 1)
             first = jnp.where(slot == k, value, first)
@@ -102,7 +131,16 @@
 
     partner = (1 - pair, row, col)
     low = pl.ds(0, columns)
-    to_partner = copy(0, feat, other.at[pl.ds(2, height), :, low], partner)
+    piece = height // CHUNKS
+    to_partner = [
+        copy(
+            12 + n if n else 0,
+            feat.at[pl.ds(n * piece, piece)],
+            other.at[pl.ds(2 + n * piece, piece), :, low],
+            partner,
+        )
+        for n in range(CHUNKS)
+    ]
     near = []
     for n, (dr, dc) in enumerate(STRIPS):
         near.append(
@@ -126,7 +164,8 @@
 
     for moved, (dr, dc), _ in near:
         pl.when(exists(dr, dc))(moved.start)
-    to_partner.start()
+    for moved in to_partner:
+        moved.start()
     for _, (dr, dc), place in near:
 
         @pl.when(jnp.logical_not(exists(-dr, -dc)))
@@ -135,8 +174,13 @@
 
     own[pl.ds(MARGIN, height), :, low] = feat[...]
 
-    w_one = jnp.concatenate([w_first[pl.ds(192 * a, 192), :] for a in range(3)], axis=1)
-    w_two = jnp.concatenate([w_second[pl.ds(192 * a, 192), :] for a in range(3)], axis=1)
+    for load in loads[1:]:
+        load.wait()
+    taps = 3 * channels
+    w_own, w_other, w_two = (
+        jnp.concatenate([ref[pl.ds(taps * a, taps), pl.ds(at, channels)] for a in range(3)], axis=1)
+        for ref, at in ((w_first, 0), (w_first, channels), (w_second, 0))
+    )
 
     for moved, (dr, dc), _ in near:
         pl.when(exists(-dr, -dc))(moved.wait_recv)
@@ -176,17 +220,24 @@
     ]
     for moved in passed:
         moved.start()
-    to_partner.wait_recv()
-    for moved in passed:
-        moved.wait_recv()
+    wide = 2 * columns
+
+    def own_part(step, carry):
+        for part in range(6):
+            y = step * 6 + part
+            window = own[pl.ds(y + MARGIN - 2, 3)].reshape(taps, wide)
+            partial[y] = jnp.dot(w_own, window, preferred_element_type=jnp.float32)
+        return carry
+
+    lax.fori_loop(0, (height + 2) // 6, own_part, 0)
+
+    passed[0].wait_recv()
     bundle = package[1].astype(jnp.float32)
     for j in range(height + 4):
         other[j, :, pl.ds(columns, columns)] = pltpu.roll(
             bundle, (2 * columns - 2 - 4 * j) % columns, 1
         ).astype(jnp.bfloat16)
 
-    wide = 2 * columns
-
     def joined_taps(z):
         return (
             pltpu.roll(z[:channels], 1, 1)
@@ -198,28 +249,30 @@
     place_col = jnp.where(wide_lane < wide * 3 // 4, wide_lane, wide_lane - wide) + col * columns
     col_ok = jnp.logical_and(place_col >= 0, place_col < n_col * columns)
 
-    def first_layer(step, carry):
-        for part in range(3):
-            y = step * 3 + part
-            window = jnp.concatenate(
-                [
-                    piece
-                    for a in range(3)
-                    for piece in (own[y + MARGIN - 2 + a], other[y + a])
-                ],
-                axis=0,
-            )
-            value = joined_taps(jnp.dot(w_one, window, preferred_element_type=jnp.float32))
-            place_row = row * height + y - 1
-            row_ok = jnp.logical_and(place_row >= 0, place_row < n_row * height)
-            ok = jnp.logical_and(col_ok, row_ok)
-            hidden[y] = jnp.where(ok, jnp.maximum(value, 0.0), 0.0).astype(jnp.bfloat16)
-        return carry
-
-    lax.fori_loop(0, (height + 2) // 3, first_layer, 0)
+    def first_layer(y):
+        window = other[pl.ds(y, 3)].reshape(taps, wide)
+        value = joined_taps(
+            partial[y] + jnp.dot(w_other, window, preferred_element_type=jnp.float32)
+        )
+        if y == 0:
+            ok = jnp.logical_and(col_ok, row > 0)
+        elif y == height + 1:
+            ok = jnp.logical_and(col_ok, row < n_row - 1)
+        else:
+            ok = col_ok
+        hidden[y] = jnp.where(ok, jnp.maximum(value, 0.0), 0.0).astype(jnp.bfloat16)
+
+    passed[1].wait_recv()
+    for n in range(CHUNKS):
+        to_partner[n].wait_recv()
+        for y in range(n * piece, (n + 1) * piece):
+            first_layer(y)
+    passed[2].wait_recv()
+    for y in range(height, height + 2):
+        first_layer(y)
 
     for y in range(height):
-        window = jnp.concatenate([hidden[y + a] for a in range(3)], axis=0)
+        window = hidden[pl.ds(y, 3)].reshape(taps, wide)
         value = joined_taps(jnp.dot(w_two, window, preferred_element_type=jnp.float32))
         hidden_two[:, pl.ds(y * columns, columns)] = jnp.maximum(value[:, :columns], 0.0).astype(
             jnp.bfloat16
@@ -255,8 +308,7 @@
     target_row = (target // columns).astype(jnp.float32)
     reach = lax.broadcasted_iota(jnp.int32, (depth, wide), 0).astype(jnp.float32) - MARGIN
 
-    def warp(t, carry):
-        y = 2 * t
+    def warp(y):
         both = [
             jnp.concatenate(
                 [motion_out[k, pl.ds(y, 1), :], motion_out[k, pl.ds(y + 1, 1), :]], axis=1
@@ -273,32 +325,34 @@
         for d in range(depth):
             term = picked[d * channels : (d + 1) * channels] * row_weight[d : d + 1]
             total = term if total is None else total + term
-        total = total.astype(jnp.bfloat16)
-        out[y] = total[:, :columns]
-        out[y + 1] = total[:, columns:]
+        flat[pl.ds(y, channels, stride=height), :] = total[:, :columns]
+        flat[pl.ds(y + 1, channels, stride=height), :] = total[:, columns:]
+
+    def warp_four(t, carry):
+        warp(4 * t)
+        warp(4 * t + 2)
         return carry
 
-    lax.fori_loop(0, height // 2, warp, 0)
+    lax.fori_loop(0, height // 4, warp_four, 0)
+    out[...] = flat[...].reshape(channels, height, columns).astype(jnp.bfloat16)
 
     for moved, (dr, dc), _ in near:
         pl.when(exists(dr, dc))(moved.wait_send)
-    to_partner.wait_send()
-    for moved in passed:
+    for moved in to_partner + passed:
         moved.wait_send()
 
 
 def shards(n_row, n_col, features, offsets, fractions, tissue, w_first, w_second, head_weight):
     _, channels, height, columns = features.shape
-    feat = jnp.transpose(features[0], (1, 0, 2))
     wide = 2 * columns
     vmem = pl.BlockSpec(memory_space=pltpu.VMEM)
     warped, motion = pl.pallas_call(
         functools.partial(kernel, n_row, n_col),
         out_shape=(
-            jax.ShapeDtypeStruct((height, channels, columns), jnp.bfloat16),
+            jax.ShapeDtypeStruct((channels, height, columns), jnp.bfloat16),
             jax.ShapeDtypeStruct((2, height, columns), jnp.float32),
         ),
-        in_specs=[vmem] * 7,
+        in_specs=[pl.BlockSpec(memory_space=pltpu.HBM)] * 5 + [vmem] * 2,
         out_specs=(vmem, vmem),
         scratch_shapes=[
             pltpu.VMEM((height + 2 * MARGIN, channels, wide), jnp.bfloat16),
@@ -308,25 +362,34 @@
             pltpu.VMEM((2, channels, columns), jnp.bfloat16),
             pltpu.VMEM((height + 2, channels, wide), jnp.bfloat16),
             pltpu.VMEM((channels, height * columns), jnp.bfloat16),
+            pltpu.VMEM((height + 2, 3 * channels, wide), jnp.float32),
+            pltpu.VMEM((channels * height, columns), jnp.float32),
+            pltpu.VMEM((height, channels, columns), jnp.bfloat16),
+            pltpu.VMEM((channels, height, columns), jnp.bfloat16),
+            pltpu.VMEM((2, height, columns), jnp.int32),
+            pltpu.VMEM((2, height, columns), jnp.int32),
+            pltpu.VMEM((9 * channels, 2 * channels), jnp.bfloat16),
+            pltpu.VMEM((9 * channels, channels), jnp.bfloat16),
             pltpu.SemaphoreType.DMA((N_COPIES,)),
             pltpu.SemaphoreType.DMA((N_COPIES,)),
+            pltpu.SemaphoreType.DMA((5,)),
         ],
         compiler_params=pltpu.CompilerParams(
-            collective_id=0, has_side_effects=True, vmem_limit_bytes=48 * 1024 * 1024
+            collective_id=0, has_side_effects=True, vmem_limit_bytes=63 * 1024 * 1024
         ),
         cost_estimate=pl.CostEstimate(
             flops=4 * 10**9, bytes_accessed=2 * 10**6, transcendentals=4096
         ),
     )(
-        feat,
+        features[0],
         offsets[0],
         fractions[0],
-        tissue[0],
         w_first.reshape(-1, w_first.shape[-1]),
         w_second.reshape(-1, w_second.shape[-1]),
+        tissue[0],
         head_weight,
     )
-    return (jnp.transpose(warped, (1, 0, 2))[None], motion[None])
+    return (warped[None], motion[None])
 
 
 def solution(mesh):

time: 23.9 us -> 22.3 us (0.933); the launches traced: 23.8 us -> 21.9 us
  local copies, waits for them, and re-layouts: 3.2 us -> 2.28 us
  Pallas kernels: 19.8 us -> 19 us
    unnamed x15 -> x4, local copies, waits for them, and re-layouts: 3.2 us -> 2.28 us
    pallas_call x1, Pallas kernels: 19.8 us -> 19 us  [shards(): pl.pallas_call(functools.partial(kernel, n_row, n_col), out_shape=(jax.Sh...]
where the time goes in v2:
time: 22.3 us; the launch traced here: 21.9 us
  Pallas kernels  19 us (85%)
  local copies, waits for them, and re-layouts  2.28 us (10%)
  between operations  0.65 us (3%)
    pallas_call x1, Pallas kernels, shards(): pl.pallas_call(functools.partial(kernel, n_row, n_col), out_shape=(jax.Sh...  19 us
    unnamed x4, local copies, waits for them, and re-layouts  2.28 us

profile of v2, /device:TPU:0, one launch (start us, length us, event | category | flops | bytes accessed | tf_op | source)
XLA Modules:
  0.0 21.9 jit_solution(3203373759358589461)
XLA Ops:
  0.6 19.0 %shard_map.86 = (bf16[64,16,128]{2,1,0:T(8,128)(2,1)}, f32[2,16,128]{2,1,0:T(8,128)}) custom-call(bf16[64,16,128]{2,1,0:T(8,128)(2,1)} %bitcast.10, s32[2,16,128]{2,1,0:T(8,128)} %bitcast.13, s32[2,16,128]{2,1,0:T(8,128)} %bitcast.14, bf16[576,128]{1,0:T(8,128)(2,1)} %bitcast.11, bf16[576,64]{1,0:T(8,128)(2,1)} %bitcast.12, s32[2,16]{1,0:T(2,128)} %bitcast.15, ...), custom_call_target="tpu_custom_call" | custom-call | flops 4000000000 | bytes 2000000 | tf_op jit(solution)/shard_map/pallas_call | solution.py:349
  19.6 0.0 copy-start
  19.6 1.7 %copy.11 = bf16[1,64,16,128]{3,2,1,0:T(8,128)(2,1)} copy(bf16[1,64,16,128]{3,2,1,0:T(8,128)(2,1)} %bitcast.8) | data formatting | bytes 524288
  21.3 0.0 copy-done
  21.3 0.6 %copy.12 = f32[1,2,16,128]{3,2,1,0:T(8,128)} copy(f32[1,2,16,128]{3,2,1,0:T(8,128)S(1)} %bitcast.9) | data formatting | bytes 32768
Async XLA Ops:
  19.6 1.7 %copy-start = (f32[2,16,128]{2,1,0:T(8,128)S(1)}, f32[2,16,128]{2,1,0:T(8,128)}, u32[]{:S(2)}) copy-start(f32[2,16,128]{2,1,0:T(8,128)} %get-tuple-element.5) | copy-start | bytes 49156

commit v3 on v2

--- a/solution.py
+++ b/solution.py
@@ -15,8 +15,8 @@
 MESH = pl.DeviceIdType.MESH
 
 STRIPS = [(dr, dc) for dr in (-1, 0, 1) for dc in (-1, 1)]
-N_COPIES = 16
-CHUNKS = 4
+N_COPIES = 14
+CHUNKS = 2
 
 
 def lanes(shape):
@@ -43,6 +43,7 @@
     hidden,
     hidden_two,
     partial,
+    residual,
     flat,
     feat,
     feat_here,
@@ -55,6 +56,7 @@
     load_sem,
 ):
     height, channels, columns = feat.shape
+    half = height // 2
     loads = [
         pltpu.make_async_copy(source, target, load_sem.at[n])
         for n, (source, target) in enumerate(
@@ -131,12 +133,15 @@
 
     partner = (1 - pair, row, col)
     low = pl.ds(0, columns)
-    piece = height // CHUNKS
+    top = pl.multiple_of(pair * half, half)
+    top_there = pl.multiple_of((1 - pair) * half, half)
+    body = half + 2
+    piece = body // CHUNKS
     to_partner = [
         copy(
             12 + n if n else 0,
-            feat.at[pl.ds(n * piece, piece)],
-            other.at[pl.ds(2 + n * piece, piece), :, low],
+            feat.at[pl.ds((1 - pair) * (height - body) + n * piece, piece)],
+            other.at[pl.ds(2 * pair + n * piece, piece), :, low],
             partner,
         )
         for n in range(CHUNKS)
@@ -177,10 +182,12 @@
     for load in loads[1:]:
         load.wait()
     taps = 3 * channels
-    w_own, w_other, w_two = (
+    w_self, w_cross, w_two = (
         jnp.concatenate([ref[pl.ds(taps * a, taps), pl.ds(at, channels)] for a in range(3)], axis=1)
         for ref, at in ((w_first, 0), (w_first, channels), (w_second, 0))
     )
+    w_own = jnp.concatenate([w_self, w_cross], axis=0)
+    w_other = jnp.concatenate([w_cross, w_self], axis=0)
 
     for moved, (dr, dc), _ in near:
         pl.when(exists(-dr, -dc))(moved.wait_recv)
@@ -207,14 +214,8 @@
         copy(9, package.at[0], package.at[1], partner),
         copy(
             10,
-            own.at[pl.ds(MARGIN - 2, 2), :, low],
-            other.at[pl.ds(0, 2), :, low],
-            partner,
-        ),
-        copy(
-            11,
-            own.at[pl.ds(MARGIN + height, 2), :, low],
-            other.at[pl.ds(height + 2, 2), :, low],
+            own.at[pl.ds(MARGIN - 2 + (1 - pair) * (height + 2), 2), :, low],
+            other.at[pl.ds((1 - pair) * body, 2), :, low],
             partner,
         ),
     ]
@@ -223,17 +224,18 @@
     wide = 2 * columns
 
     def own_part(step, carry):
-        for part in range(6):
-            y = step * 6 + part
-            window = own[pl.ds(y + MARGIN - 2, 3)].reshape(taps, wide)
+        for part in range(5):
+            y = step * 5 + part
+            window = own[pl.ds(top + y + MARGIN - 2, 3)].reshape(taps, wide)
             partial[y] = jnp.dot(w_own, window, preferred_element_type=jnp.float32)
         return carry
 
-    lax.fori_loop(0, (height + 2) // 6, own_part, 0)
+    lax.fori_loop(0, (half + 2) // 5, own_part, 0)
 
     passed[0].wait_recv()
     bundle = package[1].astype(jnp.float32)
-    for j in range(height + 4):
+    bundle = jnp.where(pair == 0, bundle, pltpu.roll(bundle, columns - 4 * half, 1))
+    for j in range(half + 4):
         other[j, :, pl.ds(columns, columns)] = pltpu.roll(
             bundle, (2 * columns - 2 - 4 * j) % columns, 1
         ).astype(jnp.bfloat16)
@@ -251,36 +253,43 @@
 
     def first_layer(y):
         window = other[pl.ds(y, 3)].reshape(taps, wide)
-        value = joined_taps(
-            partial[y] + jnp.dot(w_other, window, preferred_element_type=jnp.float32)
-        )
+        both = partial[y] + jnp.dot(w_other, window, preferred_element_type=jnp.float32)
         if y == 0:
-            ok = jnp.logical_and(col_ok, row > 0)
-        elif y == height + 1:
-            ok = jnp.logical_and(col_ok, row < n_row - 1)
+            ok = jnp.logical_and(col_ok, row * height + top > 0)
+        elif y == half + 1:
+            ok = jnp.logical_and(col_ok, row * height + top + half < n_row * height)
         else:
             ok = col_ok
-        hidden[y] = jnp.where(ok, jnp.maximum(value, 0.0), 0.0).astype(jnp.bfloat16)
+        for section in range(2):
+            value = joined_taps(both[section * taps : (section + 1) * taps])
+            hidden[section, y] = jnp.where(ok, jnp.maximum(value, 0.0), 0.0).astype(jnp.bfloat16)
 
     passed[1].wait_recv()
-    for n in range(CHUNKS):
-        to_partner[n].wait_recv()
-        for y in range(n * piece, (n + 1) * piece):
-            first_layer(y)
-    passed[2].wait_recv()
-    for y in range(height, height + 2):
+    to_partner[0].wait_recv()
+    for y in range(piece - 2):
         first_layer(y)
-
-    for y in range(height):
-        window = hidden[pl.ds(y, 3)].reshape(taps, wide)
-        value = joined_taps(jnp.dot(w_two, window, preferred_element_type=jnp.float32))
-        hidden_two[:, pl.ds(y * columns, columns)] = jnp.maximum(value[:, :columns], 0.0).astype(
-            jnp.bfloat16
-        )
-
-    residual = jnp.tanh(
-        jnp.dot(head[...], hidden_two[...], preferred_element_type=jnp.float32)
-    )
+    for moved in to_partner[1:]:
+        moved.wait_recv()
+    for y in range(piece - 2, half + 2):
+        first_layer(y)
+
+    back = copy(11, residual.at[1], residual.at[2], partner)
+    for section in (1, 0):
+        for y in range(half):
+            window = hidden[section, pl.ds(y, 3)].reshape(taps, wide)
+            value = joined_taps(jnp.dot(w_two, window, preferred_element_type=jnp.float32))
+            hidden_two[:, pl.ds(y * columns, columns)] = jnp.maximum(
+                value[:, :columns], 0.0
+            ).astype(jnp.bfloat16)
+        value = jnp.tanh(jnp.dot(head[...], hidden_two[...], preferred_element_type=jnp.float32))
+        for y in range(half):
+            for k in range(2):
+                residual[section, k, pl.ds(y, 1), :] = value[
+                    k : k + 1, y * columns : (y + 1) * columns
+                ]
+        if section:
+            back.start()
+
     cells = columns // BLK
     spread = (
         lax.broadcasted_iota(jnp.int32, (cells, columns), 1) // BLK
@@ -291,13 +300,24 @@
         spread,
         preferred_element_type=jnp.float32,
     )
-    for y in range(height):
-        cover = coverage[y // BLK : y // BLK + 1]
+
+    def move(start, place, upper):
+        cover = [
+            jnp.broadcast_to(
+                jnp.where(
+                    upper, coverage[n : n + 1], coverage[half // BLK + n : half // BLK + n + 1]
+                ),
+                (BLK, columns),
+            )
+            for n in range(half // BLK)
+        ]
+        cover = jnp.concatenate(cover, axis=0) if len(cover) > 1 else cover[0]
+        rows = pl.ds(start, half)
         for k in range(2):
-            motion_out[k, pl.ds(y, 1), :] = (
-                offsets[k, pl.ds(y, 1), :].astype(jnp.float32)
-                + fractions[k, pl.ds(y, 1), :].astype(jnp.float32) / FRAC_SCALE
-                + cover * residual[k : k + 1, y * columns : (y + 1) * columns]
+            motion_out[k, rows, :] = (
+                offsets[k, rows, :].astype(jnp.float32)
+                + fractions[k, rows, :].astype(jnp.float32) / FRAC_SCALE
+                + cover * residual[place, k]
             )
 
     depth = 2 * MARGIN + 2
@@ -328,17 +348,22 @@
         flat[pl.ds(y, channels, stride=height), :] = total[:, :columns]
         flat[pl.ds(y + 1, channels, stride=height), :] = total[:, columns:]
 
-    def warp_four(t, carry):
-        warp(4 * t)
-        warp(4 * t + 2)
-        return carry
-
-    lax.fori_loop(0, height // 4, warp_four, 0)
+    for start, place, upper in ((top, 0, pair == 0), (top_there, 2, pair != 0)):
+        if place:
+            back.wait_recv()
+        move(start, place, upper)
+
+        def warp_four(t, carry):
+            warp(start + 4 * t)
+            warp(start + 4 * t + 2)
+            return carry
+
+        lax.fori_loop(0, half // 4, warp_four, 0)
     out[...] = flat[...].reshape(channels, height, columns).astype(jnp.bfloat16)
 
     for moved, (dr, dc), _ in near:
         pl.when(exists(dr, dc))(moved.wait_send)
-    for moved in to_partner + passed:
+    for moved in to_partner + passed + [back]:
         moved.wait_send()
 
 
@@ -356,13 +381,14 @@
         out_specs=(vmem, vmem),
         scratch_shapes=[
             pltpu.VMEM((height + 2 * MARGIN, channels, wide), jnp.bfloat16),
-            pltpu.VMEM((height + 4, channels, wide), jnp.bfloat16),
+            pltpu.VMEM((height // 2 + 4, channels, wide), jnp.bfloat16),
             pltpu.VMEM((2, 2, channels, columns), jnp.bfloat16),
             pltpu.VMEM((6, 2, channels, columns), jnp.bfloat16),
             pltpu.VMEM((2, channels, columns), jnp.bfloat16),
-            pltpu.VMEM((height + 2, channels, wide), jnp.bfloat16),
-            pltpu.VMEM((channels, height * columns), jnp.bfloat16),
-            pltpu.VMEM((height + 2, 3 * channels, wide), jnp.float32),
+            pltpu.VMEM((2, height // 2 + 2, channels, wide), jnp.bfloat16),
+            pltpu.VMEM((channels, height // 2 * columns), jnp.bfloat16),
+            pltpu.VMEM((height // 2 + 2, 6 * channels, wide), jnp.float32),
+            pltpu.VMEM((3, 2, height // 2, columns), jnp.float32),
             pltpu.VMEM((channels * height, columns), jnp.float32),
             pltpu.VMEM((height, channels, columns), jnp.bfloat16),
             pltpu.VMEM((channels, height, columns), jnp.bfloat16),

time: 22.3 us -> 21.7 us (0.973)
  Pallas kernels: 19 us -> 18.6 us
    pallas_call x1, Pallas kernels: 19 us -> 18.6 us  [shards(): pl.pallas_call(functools.partial(kernel, n_row, n_col), out_shape=(jax.Sh...]
where the time goes in v3:
time: 21.7 us; the launch traced here: 21.5 us
  Pallas kernels  18.6 us (86%)
  local copies, waits for them, and re-layouts  2.28 us (11%)
  between operations  0.65 us (3%)
    pallas_call x1, Pallas kernels, shards(): pl.pallas_call(functools.partial(kernel, n_row, n_col), out_shape=(jax.Sh...  18.6 us
    unnamed x4, local copies, waits for them, and re-layouts  2.28 us

profile of v3, /device:TPU:0, one launch (start us, length us, event | category | flops | bytes accessed | tf_op | source)
XLA Modules:
  0.0 21.5 jit_solution(10782807395723486907)
XLA Ops:
  0.6 18.6 %shard_map.86 = (bf16[64,16,128]{2,1,0:T(8,128)(2,1)}, f32[2,16,128]{2,1,0:T(8,128)}) custom-call(bf16[64,16,128]{2,1,0:T(8,128)(2,1)} %bitcast.10, s32[2,16,128]{2,1,0:T(8,128)} %bitcast.13, s32[2,16,128]{2,1,0:T(8,128)} %bitcast.14, bf16[576,128]{1,0:T(8,128)(2,1)} %bitcast.11, bf16[576,64]{1,0:T(8,128)(2,1)} %bitcast.12, s32[2,16]{1,0:T(2,128)} %bitcast.15, ...), custom_call_target="tpu_custom_call" | custom-call | flops 4000000000 | bytes 2000000 | tf_op jit(solution)/shard_map/pallas_call | solution.py:374
  19.2 0.0 copy-start
  19.2 1.7 %copy.11 = bf16[1,64,16,128]{3,2,1,0:T(8,128)(2,1)} copy(bf16[1,64,16,128]{3,2,1,0:T(8,128)(2,1)} %bitcast.8) | data formatting | bytes 524288
  20.9 0.0 copy-done
  20.9 0.6 %copy.12 = f32[1,2,16,128]{3,2,1,0:T(8,128)} copy(f32[1,2,16,128]{3,2,1,0:T(8,128)S(1)} %bitcast.9) | data formatting | bytes 32768
Async XLA Ops:
  19.2 1.7 %copy-start = (f32[2,16,128]{2,1,0:T(8,128)S(1)}, f32[2,16,128]{2,1,0:T(8,128)}, u32[]{:S(2)}) copy-start(f32[2,16,128]{2,1,0:T(8,128)} %get-tuple-element.5) | copy-start | bytes 49156

commit v4 on v3

--- a/solution.py
+++ b/solution.py
@@ -374,8 +374,8 @@
     warped, motion = pl.pallas_call(
         functools.partial(kernel, n_row, n_col),
         out_shape=(
-            jax.ShapeDtypeStruct((channels, height, columns), jnp.bfloat16),
-            jax.ShapeDtypeStruct((2, height, columns), jnp.float32),
+            pltpu.VMEM((channels, height, columns), jnp.bfloat16),
+            pltpu.VMEM((2, height, columns), jnp.float32),
         ),
         in_specs=[pl.BlockSpec(memory_space=pltpu.HBM)] * 5 + [vmem] * 2,
         out_specs=(vmem, vmem),

time: 21.7 us -> 20 us (0.922)
  local copies, waits for them, and re-layouts: 2.28 us -> 1.31 us
  Pallas kernels: 18.6 us -> 17.9 us
    unnamed x4 -> x2, local copies, waits for them, and re-layouts: 2.28 us -> 1.31 us
    pallas_call x1, Pallas kernels: 18.6 us -> 17.9 us  [shards(): pl.pallas_call(functools.partial(kernel, n_row, n_col), out_shape=(pltpu....]
where the time goes in v4:
time: 20 us; the launch traced here: 19.9 us
  Pallas kernels  17.9 us (89%)
  local copies, waits for them, and re-layouts  1.31 us (7%)
  between operations  0.64 us (3%)
    pallas_call x1, Pallas kernels, shards(): pl.pallas_call(functools.partial(kernel, n_row, n_col), out_shape=(pltpu....  17.9 us
    unnamed x2, local copies, waits for them, and re-layouts  1.31 us

profile of v4, /device:TPU:0, one launch (start us, length us, event | category | flops | bytes accessed | tf_op | source)
XLA Modules:
  0.0 19.9 jit_solution(10379387659952041288)
XLA Ops:
  0.6 17.9 %shard_map.86 = (bf16[64,16,128]{2,1,0:T(8,128)(2,1)S(1)}, f32[2,16,128]{2,1,0:T(8,128)S(1)}) custom-call(bf16[64,16,128]{2,1,0:T(8,128)(2,1)} %bitcast.10, s32[2,16,128]{2,1,0:T(8,128)} %bitcast.13, s32[2,16,128]{2,1,0:T(8,128)} %bitcast.14, bf16[576,128]{1,0:T(8,128)(2,1)} %bitcast.11, bf16[576,64]{1,0:T(8,128)(2,1)} %bitcast.12, s32[2,16]{1,0:T(2,128)} %bitcast.15, ...), custom_call_target="tpu_custom_call" | custom-call | flops 4000000000 | bytes 2000000 | tf_op jit(solution)/shard_map/pallas_call | solution.py:374
  18.5 0.7 %copy.11 = bf16[1,64,16,128]{3,2,1,0:T(8,128)(2,1)} copy(bf16[1,64,16,128]{3,2,1,0:T(8,128)(2,1)S(1)} %bitcast.8) | data formatting | bytes 524288
  19.2 0.6 %copy.12 = f32[1,2,16,128]{3,2,1,0:T(8,128)} copy(f32[1,2,16,128]{3,2,1,0:T(8,128)S(1)} %bitcast.9) | data formatting | bytes 32768

commit v5 on v4

--- a/solution.py
+++ b/solution.py
@@ -192,24 +192,6 @@
     for moved, (dr, dc), _ in near:
         pl.when(exists(-dr, -dc))(moved.wait_recv)
 
-    bundle = jnp.zeros((channels, columns), jnp.float32)
-    for i in range(height + 2 * MARGIN):
-        side = -1 if i < MARGIN else (0 if i < MARGIN + height else 1)
-        k = i - MARGIN - side * height
-        left = strips[STRIPS.index((-side, 1)), k // slots].astype(jnp.float32)
-        right = strips[STRIPS.index((-side, -1)), k // slots].astype(jnp.float32)
-        k = k % slots
-        value = jnp.where(
-            slot == k, right, jnp.where(slot == (k - 1) % slots, left, 0.0)
-        )
-        if k:
-            value = pltpu.roll(value, columns - STRIP * k, 1)
-        own[i, :, pl.ds(columns, columns)] = value.astype(jnp.bfloat16)
-        j = i - MARGIN + 2
-        if 0 <= j < height + 4:
-            bundle = jnp.where(lane // 4 == j, pltpu.roll(value, 2 + 4 * j, 1), bundle)
-    package[0] = bundle.astype(jnp.bfloat16)
-
     passed = [
         copy(9, package.at[0], package.at[1], partner),
         copy(
@@ -219,8 +201,33 @@
             partner,
         ),
     ]
-    for moved in passed:
-        moved.start()
+    passed[1].start()
+
+    bundle = jnp.zeros((channels, columns), jnp.float32)
+    needed = range(MARGIN - 2, MARGIN + height + 2)
+
+    def unpack(i):
+        side = -1 if i < MARGIN else (0 if i < MARGIN + height else 1)
+        k = i - MARGIN - side * height
+        left = strips[STRIPS.index((-side, 1)), k // slots].astype(jnp.float32)
+        right = strips[STRIPS.index((-side, -1)), k // slots].astype(jnp.float32)
+        k = k % slots
+        value = jnp.where(
+            slot == k, right, jnp.where(slot == (k - 1) % slots, left, 0.0)
+        )
+        if k:
+            value = pltpu.roll(value, columns - STRIP * k, 1)
+        own[i, :, pl.ds(columns, columns)] = value.astype(jnp.bfloat16)
+        return value
+
+    for j, i in enumerate(needed):
+        bundle = jnp.where(lane // 4 == j, pltpu.roll(unpack(i), 2 + 4 * j, 1), bundle)
+    package[0] = bundle.astype(jnp.bfloat16)
+
+    passed[0].start()
+    for i in range(height + 2 * MARGIN):
+        if i not in needed:
+            unpack(i)
     wide = 2 * columns
 
     def own_part(step, carry):
@@ -352,13 +359,8 @@
         if place:
             back.wait_recv()
         move(start, place, upper)
-
-        def warp_four(t, carry):
-            warp(start + 4 * t)
-            warp(start + 4 * t + 2)
-            return carry
-
-        lax.fori_loop(0, half // 4, warp_four, 0)
+        for t in range(half // 2):
+            warp(start + 2 * t)
     out[...] = flat[...].reshape(channels, height, columns).astype(jnp.bfloat16)
 
     for moved, (dr, dc), _ in near:

time: 20 us -> 19.1 us (0.955)
  Pallas kernels: 17.9 us -> 17 us
    pallas_call x1, Pallas kernels: 17.9 us -> 17 us  [shards(): pl.pallas_call(functools.partial(kernel, n_row, n_col), out_shape=(pltpu....]
where the time goes in v5:
time: 19.1 us; the launch traced here: 18.9 us
  Pallas kernels  17 us (89%)
  local copies, waits for them, and re-layouts  1.31 us (7%)
  between operations  0.64 us (3%)
    pallas_call x1, Pallas kernels, shards(): pl.pallas_call(functools.partial(kernel, n_row, n_col), out_shape=(pltpu....  17 us
    unnamed x2, local copies, waits for them, and re-layouts  1.31 us

profile of v5, /device:TPU:0, one launch (start us, length us, event | category | flops | bytes accessed | tf_op | source)
XLA Modules:
  0.0 18.9 jit_solution(2500436579742595354)
XLA Ops:
  0.6 17.0 %shard_map.86 = (bf16[64,16,128]{2,1,0:T(8,128)(2,1)S(1)}, f32[2,16,128]{2,1,0:T(8,128)S(1)}) custom-call(bf16[64,16,128]{2,1,0:T(8,128)(2,1)} %bitcast.10, s32[2,16,128]{2,1,0:T(8,128)} %bitcast.13, s32[2,16,128]{2,1,0:T(8,128)} %bitcast.14, bf16[576,128]{1,0:T(8,128)(2,1)} %bitcast.11, bf16[576,64]{1,0:T(8,128)(2,1)} %bitcast.12, s32[2,16]{1,0:T(2,128)} %bitcast.15, ...), custom_call_target="tpu_custom_call" | custom-call | flops 4000000000 | bytes 2000000 | tf_op jit(solution)/shard_map/pallas_call | solution.py:376
  17.6 0.7 %copy.11 = bf16[1,64,16,128]{3,2,1,0:T(8,128)(2,1)} copy(bf16[1,64,16,128]{3,2,1,0:T(8,128)(2,1)S(1)} %bitcast.8) | data formatting | bytes 524288
  18.3 0.6 %copy.12 = f32[1,2,16,128]{3,2,1,0:T(8,128)} copy(f32[1,2,16,128]{3,2,1,0:T(8,128)S(1)} %bitcast.9) | data formatting | bytes 32768

commit v6 on v5

--- a/solution.py
+++ b/solution.py
@@ -167,10 +167,10 @@
         place = own.at[target, :, low]
         near.append((copy(index, feat.at[source], place, (pair, row + dr, col)), (dr, 0), place))
 
+    for moved in to_partner:
+        moved.start()
     for moved, (dr, dc), _ in near:
         pl.when(exists(dr, dc))(moved.start)
-    for moved in to_partner:
-        moved.start()
     for _, (dr, dc), place in near:
 
         @pl.when(jnp.logical_not(exists(-dr, -dc)))

time: 19.1 us -> 19.1 us (level)
  no operation moved by 1% of the time
where the time goes in v6:
time: 19.1 us; the launch traced here: 18.9 us
  Pallas kernels  17 us (89%)
  local copies, waits for them, and re-layouts  1.31 us (7%)
  between operations  0.64 us (3%)
    pallas_call x1, Pallas kernels, shards(): pl.pallas_call(functools.partial(kernel, n_row, n_col), out_shape=(pltpu....  17 us
    unnamed x2, local copies, waits for them, and re-layouts  1.31 us

profile of v6, /device:TPU:0, one launch (start us, length us, event | category | flops | bytes accessed | tf_op | source)
XLA Modules:
  0.0 18.9 jit_solution(14836654811047153180)
XLA Ops:
  0.6 17.0 %shard_map.86 = (bf16[64,16,128]{2,1,0:T(8,128)(2,1)S(1)}, f32[2,16,128]{2,1,0:T(8,128)S(1)}) custom-call(bf16[64,16,128]{2,1,0:T(8,128)(2,1)} %bitcast.10, s32[2,16,128]{2,1,0:T(8,128)} %bitcast.13, s32[2,16,128]{2,1,0:T(8,128)} %bitcast.14, bf16[576,128]{1,0:T(8,128)(2,1)} %bitcast.11, bf16[576,64]{1,0:T(8,128)(2,1)} %bitcast.12, s32[2,16]{1,0:T(2,128)} %bitcast.15, ...), custom_call_target="tpu_custom_call" | custom-call | flops 4000000000 | bytes 2000000 | tf_op jit(solution)/shard_map/pallas_call | solution.py:376
  17.6 0.7 %copy.11 = bf16[1,64,16,128]{3,2,1,0:T(8,128)(2,1)} copy(bf16[1,64,16,128]{3,2,1,0:T(8,128)(2,1)S(1)} %bitcast.8) | data formatting | bytes 524288
  18.3 0.6 %copy.12 = f32[1,2,16,128]{3,2,1,0:T(8,128)} copy(f32[1,2,16,128]{3,2,1,0:T(8,128)S(1)} %bitcast.9) | data formatting | bytes 32768
